TPU v7x, 32 devices: a whole 2x2x4 slice. The times are simulated.
32 devices in a mesh: parts: 2 (over y), tensor: 4 (over x, core), request: 4 (over z).
Axes of the slice: x: 2, y: 2, z: 4, core: 2. Of those that a mesh axis runs over, the one named last changes fastest.
Arguments:
- attn_heads: bfloat16 [768, 8192], P('parts', 'tensor'), parts along dimension 0, may hold values from -6 to 6
- out_weight: bfloat16 [8192, 8192], P('tensor', 'request'), may hold values from -0.0625 to 0.0625
- resid: bfloat16 [768, 8192], P(('parts', 'tensor'), 'request'), parts along dimension 0
- gain: bfloat16 [8192], P('request'), may hold values from 0.5 to 1.5
- gate_weight: bfloat16 [8192, 14336], P('request', 'tensor'), may hold values from -0.0625 to 0.0625
- up_weight: bfloat16 [8192, 14336], P('request', 'tensor'), may hold values from -0.0625 to 0.0625
- down_weight: bfloat16 [14336, 8192], P('tensor', 'request'), may hold values from -0.046875 to 0.046875
- signs: int32 [4, 8192], P(None, 'request'), may hold values from 0 to 1
- expos: int32 [4, 64], P(None, 'request'), may hold values from -12 to -8
Outputs:
- mixed: bfloat16 [768, 8192], P('parts', 'request'), parts along dimension 0
There are 2 independent parts, one for each index of `parts`. A program takes and returns all parts, laid end to end along the dimension named above; an argument that names none is the same for every part. Nothing has to cross between parts.
Inputs may be any that keep to these rules, and one draw needn't show every extreme that they name: `signs`: each entry is 0 or 1 and stands for the sign 2 s - 1.
All inputs are finite; a program needn't handle non-finite values.
Results may differ from a plain program's by a relative error of at most 0.013.
Values may be sent and summed in bfloat16 or wider, within the bound.
A program may use at most 192 MiB of HBM per device.

v0:
```python
import jax
import jax.numpy as jnp
from jax import lax
from jax.sharding import PartitionSpec as P

D = 8192


def hadamard():
    index = jnp.arange(128, dtype=jnp.int32)
    common = jnp.bitwise_and(index[:, None], index[None, :])
    ones_count = jnp.zeros((128, 128), jnp.int32)
    for level in range(7):
        ones_count = ones_count + jnp.bitwise_and(jnp.right_shift(common, level), 1)
    return (1 - 2 * (ones_count % 2)).astype(jnp.float32)


def rotate(values, sign_bits):
    shape = values.shape
    flipped = values * (2 * sign_bits - 1).astype(jnp.float32)
    turned = jnp.dot(flipped.reshape(-1, 128), hadamard(), precision=lax.Precision.HIGHEST)
    return turned.reshape(shape) * 0.125


def unrotate(values, sign_bits):
    shape = values.shape
    turned = jnp.dot(values.reshape(-1, 128), hadamard(), precision=lax.Precision.HIGHEST)
    return turned.reshape(shape) * 0.0625 * (2 * sign_bits - 1).astype(jnp.float32)


def encode(values, sign_bits, exponents, offset):
    factor = jnp.repeat(jnp.exp2(-(exponents + offset).astype(jnp.float32)), 128)
    return jnp.clip(rotate(values, sign_bits) * factor, -448.0, 448.0).astype(jnp.bfloat16)


def decode(values, sign_bits, exponents, offset):
    factor = jnp.repeat(jnp.exp2((exponents + offset).astype(jnp.float32)), 128)
    return unrotate(values * factor, sign_bits)


def activate(gate_sum, up_sum, square_sum):
    factor = lax.rsqrt(square_sum / D + 1e-05)[:, None]
    return (jax.nn.silu(factor * gate_sum) * (factor * up_sum)).astype(jnp.bfloat16)


def shards(attn_heads, out_weight, resid, gain, gate_weight, up_weight, down_weight, signs, expos):
    picked = attn_heads
    product = jnp.dot(picked, out_weight, preferred_element_type=jnp.float32)
    summed = lax.psum_scatter(
        encode(product, signs[0], expos[0], 4).astype(jnp.float32).astype(jnp.bfloat16),
        "tensor",
        scatter_dimension=0,
        tiled=True,
    ).astype(jnp.float32)
    hidden_state = resid.astype(jnp.float32) + decode(summed, signs[0], expos[0], 4)
    coded = encode(hidden_state, signs[1], expos[1], 8)
    gathered = lax.all_gather(coded, "tensor", axis=0, tiled=True)
    restored = decode(gathered.astype(jnp.float32), signs[1], expos[1], 8)
    squares = jnp.sum(restored * restored, axis=1)
    normed = (restored * gain.astype(jnp.float32)).astype(jnp.bfloat16)
    gate_part = jnp.dot(normed, gate_weight, preferred_element_type=jnp.float32)
    up_part = jnp.dot(normed, up_weight, preferred_element_type=jnp.float32)
    gate_sum, up_sum, square_sum = (
        lax.psum(gate_part.astype(jnp.bfloat16), "request").astype(jnp.float32),
        lax.psum(up_part.astype(jnp.bfloat16), "request").astype(jnp.float32),
        lax.psum(squares.astype(jnp.bfloat16), "request").astype(jnp.float32),
    )
    hidden = activate(gate_sum, up_sum, square_sum)
    picked = hidden
    product = jnp.dot(picked, down_weight, preferred_element_type=jnp.float32)
    summed_ffn = lax.psum_scatter(
        encode(product, signs[2], expos[2], 4).astype(jnp.float32).astype(jnp.bfloat16),
        "tensor",
        scatter_dimension=0,
        tiled=True,
    ).astype(jnp.float32)
    updated = hidden_state + decode(summed_ffn, signs[2], expos[2], 4)
    final_code = encode(updated, signs[3], expos[3], 6)
    final_rows = lax.all_gather(final_code, "tensor", axis=0, tiled=True)
    return decode(final_rows.astype(jnp.float32), signs[3], expos[3], 6).astype(jnp.bfloat16)


def solution(mesh):
    return jax.shard_map(
        shards,
        mesh=mesh,
        in_specs=(
            P("parts", "tensor"),
            P("tensor", "request"),
            P(("parts", "tensor"), "request"),
            P("request"),
            P("request", "tensor"),
            P("request", "tensor"),
            P("tensor", "request"),
            P(None, "request"),
            P(None, "request"),
        ),
        out_specs=P("parts", "request"),
        check_vma=False,
    )
```

profile of v0, /device:TPU:0, one launch (start us, length us, event | category | flops | bytes accessed | tf_op | source)
XLA Modules:
  0.0 423.8 jit_solution(6269471589804942943)
XLA Ops:
  9.6 8.4 %convolution_multiply_fusion.1 = f32[384,2048]{1,0:T(8,128)} fusion(bf16[384,2048]{1,0:T(8,128)(2,1)S(1)} %copy-done, bf16[2048,2048]{1,0:T(8,128)(2,1)} %param.10, f32[2048]{0:T(1024)S(1)} %bitcast.59), kind=kOutput, calls=%fused_computation.11 | convolution fusion | flops 3222011904 | bytes 13115392 | tf_op jit(solution)/shard_map/dot_general | solution.py:48
  18.0 2.8 reshape.108
  20.8 4.3 %fusion.21 = f32[6144,128]{1,0:T(8,128)} fusion(f32[6144,128]{1,0:T(8,128)S(1)} %reshape.108), kind=kOutput, calls=%fused_computation.35 | convolution fusion | flops 1208532992 | bytes 6291456 | tf_op jit(solution)/shard_map/dot_general | solution.py:21
  25.2 2.8 reshape.109
  32.3 28.2 %reduce-scatter.3.cloned.1.call-done = bf16[96,2048]{1,0:T(8,128)(2,1)} async-done(((bf16[384,2048]{1,0:T(8,128)(2,1)}), bf16[96,2048]{1,0:T(8,128)(2,1)}) %reduce-scatter.3.cloned.1.call-update) | async-done | bytes 393232 | tf_op jit(solution)/shard_map/reduce_scatter | solution.py:49
  66.0 2.4 copy.11
  71.6 13.1 %all-gather.3.cloned.1.call-done = bf16[384,2048]{1,0:T(8,128)(2,1)} async-done(((bf16[96,2048]{1,0:T(8,128)(2,1)}), bf16[384,2048]{1,0:T(8,128)(2,1)}) %all-gather.3.cloned.1.call-update) | async-done | bytes 1572880 | tf_op jit(solution)/shard_map/all_gather | solution.py:57
  88.7 8.3 %multiply_reduce_fusion = (f32[6144]{0:T(1024)}, f32[6144,128]{0,1:T(8,128)}) fusion(f32[6144,128]{0,1:T(8,128)} %copy.11, f32[6144,128]{1,0:T(8,128)} %reshape.114), kind=kOutput, calls=%fused_computation.7 | convolution fusion | flops 1210886144 | bytes 9461760 | tf_op jit(solution)/shard_map/dot_general | solution.py:27
  97.1 2.4 copy.12
  99.4 2.3 reshape.115
  101.7 11.3 %convolution_convert_fusion.1 = bf16[384,3584]{1,0:T(8,128)(2,1)} fusion(bf16[2048,3584]{1,0:T(8,128)(2,1)} %param.13, f32[384,2048]{1,0:T(8,128)} %reshape.115, f32[2048]{0:T(1024)} %convert_element_type.137, f32[2048]{0:T(1024)} %broadcast_multiply_fusion.3), kind=kOutput, calls=%fused_computation.1 | convolution fusion | flops 5640880128 | bytes 20594688 | tf_op jit(solution)/shard_map/dot_general | solution.py:61
  113.1 12.4 %convolution_convert_fusion = bf16[384,3584]{1,0:T(8,128)(2,1)} fusion(bf16[2048,3584]{1,0:T(8,128)(2,1)} %param.14, f32[384,2048]{1,0:T(8,128)S(1)} %copy-done.4, f32[2048]{0:T(1024)S(1)} %copy-done.12, f32[2048]{0:T(1024)S(1)} %copy-done.13), kind=kOutput, calls=%fused_computation | convolution fusion | flops 5640880128 | bytes 20594688 | tf_op jit(solution)/shard_map/dot_general | solution.py:62
  126.5 12.1 %psum.21 = bf16[384]{0:T(512)(128)(2,1)S(1)} all-reduce(bf16[384]{0:T(512)(128)(2,1)S(1)} %reduce_sum.18), channel_id=1, replica_groups=mesh['parts'=2,'tensor'=4,'request'=4] {'request'}, use_global_device_ids=true, to_apply=%region_3.4 | all-reduce | flops 384 | bytes 1536 | tf_op jit(solution)/shard_map/psum | solution.py:66
  138.7 184.9 %all-reduce.3.cloned.1.call-done = (bf16[384,3584]{1,0:T(8,128)(2,1)}, bf16[384,3584]{1,0:T(8,128)(2,1)}) async-done(((bf16[384,3584]{1,0:T(8,128)(2,1)}, bf16[384,3584]{1,0:T(8,128)(2,1)}), (bf16[384,3584]{1,0:T(8,128)(2,1)}, bf16[384,3584]{1,0:T(8,128)(2,1)})) %all-reduce.3.cloned.1.call-update) | async-done | bytes 5505040 | tf_op jit(solution)/shard_map/psum | solution.py:65
  323.5 13.1 %convolution_multiply_fusion = f32[384,2048]{1,0:T(8,128)} fusion(bf16[3584,2048]{1,0:T(8,128)(2,1)} %param.15, bf16[384,3584]{1,0:T(8,128)(2,1)} %get-tuple-element.5, bf16[384,3584]{1,0:T(8,128)(2,1)} %get-tuple-element.6, f32[384]{0:T(512)S(1)} %add_rsqrt_fusion, f32[2048]{0:T(1024)S(1)} %bitcast.58), kind=kOutput, calls=%fused_computation.10 | convolution fusion | flops 5651693568 | bytes 23340544 | tf_op jit(solution)/shard_map/dot_general | solution.py:70
  336.7 2.8 reshape.116
  339.5 4.3 %fusion.13 = f32[6144,128]{1,0:T(8,128)} fusion(f32[6144,128]{1,0:T(8,128)S(1)} %reshape.116), kind=kOutput, calls=%fused_computation.31 | convolution fusion | flops 1208532992 | bytes 6291456 | tf_op jit(solution)/shard_map/dot_general | solution.py:21
  343.8 2.8 reshape.117
  349.1 26.4 %reduce-scatter.5.cloned.1.call-done = bf16[96,2048]{1,0:T(8,128)(2,1)} async-done(((bf16[384,2048]{1,0:T(8,128)(2,1)}), bf16[96,2048]{1,0:T(8,128)(2,1)}) %reduce-scatter.5.cloned.1.call-update) | async-done | bytes 393232 | tf_op jit(solution)/shard_map/reduce_scatter | solution.py:71
  379.9 19.7 %all-gather.5.cloned.1.call-done = bf16[384,2048]{1,0:T(8,128)(2,1)} async-done(((bf16[96,2048]{1,0:T(8,128)(2,1)}), bf16[384,2048]{1,0:T(8,128)(2,1)}) %all-gather.5.cloned.1.call-update) | async-done | bytes 1572880 | tf_op jit(solution)/shard_map/all_gather | solution.py:79
  401.5 2.3 reshape.122
  403.8 5.5 %fusion.7 = f32[6144,128]{1,0:T(8,128)} fusion(f32[6144,128]{1,0:T(8,128)} %reshape.122), kind=kOutput, calls=%fused_computation.28 | convolution fusion | flops 1208532992 | bytes 6291456 | tf_op jit(solution)/shard_map/dot_general | solution.py:27
  409.2 4.7 %reshape.123 = f32[384,2048]{1,0:T(8,128)} reshape(f32[6144,128]{1,0:T(8,128)} %fusion.7) | data formatting | bytes 6291456 | tf_op jit(solution)/shard_map/reshape | solution.py:28
  413.9 3.4 multiply_convert_fusion.1
  (79 shorter events, 29.5 us)
Async XLA Ops:
  6.5 3.0 copy-start
  6.5 54.0 %reduce-scatter.3.cloned.1.call-start = ((), (), s32[]{:S(2)}) async-start(), calls=%async_computation.2 | async-start | bytes 1966080 | tf_op jit(solution)/shard_map/reduce_scatter | solution.py:49
  9.6 8.5 %copy-start.11 = (f32[1,2048]{1,0:T(1,128)}, f32[1,2048]{1,0:T(1,128)S(1)}, u32[]{:S(2)}) copy-start(f32[1,2048]{1,0:T(1,128)S(1)} %get-tuple-element.10) | copy-start | bytes 24580
  9.6 20.1 %copy-start.9 = (f32[1,2048]{1,0:T(1,128)}, f32[1,2048]{1,0:T(1,128)S(1)}, u32[]{:S(2)}) copy-start(f32[1,2048]{1,0:T(1,128)S(1)} %get-tuple-element.11) | copy-start | bytes 24580
  29.5 33.2 %copy-start.5 = (bf16[96,2048]{1,0:T(8,128)(2,1)S(1)}, bf16[96,2048]{1,0:T(8,128)(2,1)}, u32[]{:S(2)}) copy-start(bf16[96,2048]{1,0:T(8,128)(2,1)} %param.11) | copy-start | bytes 1179652
  29.5 55.1 %all-gather.3.cloned.1.call-start = ((), (), s32[]{:S(2)}) async-start(), calls=%async_computation.3 | async-start | bytes 1966080 | tf_op jit(solution)/shard_map/all_gather | solution.py:57
  62.7 1.3 copy-start.2
  64.8 258.7 %all-reduce.3.cloned.1.call-start = ((), (), s32[]{:S(2)}) async-start(), calls=%async_computation.6 | async-start | bytes 11010048 | tf_op jit(solution)/shard_map/psum | solution.py:65
  101.7 11.3 %copy-start.4 = (f32[384,2048]{1,0:T(8,128)S(1)}, f32[384,2048]{1,0:T(8,128)}, u32[]{:S(2)}) copy-start(f32[384,2048]{1,0:T(8,128)} %reshape.115) | copy-start | bytes 9437188
  101.7 11.3 %copy-start.12 = (f32[2048]{0:T(1024)S(1)}, f32[2048]{0:T(1024)}, u32[]{:S(2)}) copy-start(f32[2048]{0:T(1024)} %convert_element_type.137) | copy-start | bytes 24580
  101.7 11.3 %copy-start.13 = (f32[2048]{0:T(1024)S(1)}, f32[2048]{0:T(1024)}, u32[]{:S(2)}) copy-start(f32[2048]{0:T(1024)} %broadcast_multiply_fusion.3) | copy-start | bytes 24580
  125.5 0.7 copy-start.6
  125.5 198.0 %copy-start.10 = (f32[1,2048]{1,0:T(1,128)S(1)}, f32[1,2048]{1,0:T(1,128)}, u32[]{:S(2)}) copy-start(f32[1,2048]{1,0:T(1,128)} %copy-done.9) | copy-start | bytes 24580
  125.5 250.0 %reduce-scatter.5.cloned.1.call-start = ((), (), s32[]{:S(2)}) async-start(), calls=%async_computation.4 | async-start | bytes 1966080 | tf_op jit(solution)/shard_map/reduce_scatter | solution.py:71
  348.2 29.5 %copy-start.3 = (f32[96,2048]{1,0:T(8,128)S(1)}, f32[96,2048]{1,0:T(8,128)}, u32[]{:S(2)}) copy-start(f32[96,2048]{1,0:T(8,128)} %copy-done.2) | copy-start | bytes 2359300
  348.2 29.5 %copy-start.7 = (f32[1,2048]{1,0:T(1,128)S(1)}, f32[1,2048]{1,0:T(1,128)}, u32[]{:S(2)}) copy-start(f32[1,2048]{1,0:T(1,128)} %get-tuple-element.9) | copy-start | bytes 24580
  348.2 29.5 %copy-start.8 = (f32[2048]{0:T(1024)S(1)}, f32[2048]{0:T(1024)}, u32[]{:S(2)}) copy-start(f32[2048]{0:T(1024)} %get-tuple-element.28) | copy-start | bytes 24580
  348.2 51.5 %all-gather.5.cloned.1.call-start = ((), (), s32[]{:S(2)}) async-start(), calls=%async_computation.5 | async-start | bytes 1966080 | tf_op jit(solution)/shard_map/all_gather | solution.py:79
  377.9 2.0 copy-start.14
  409.2 8.1 %copy-start.1 = (bf16[384,2048]{1,0:T(8,128)(2,1)S(1)}, bf16[384,2048]{1,0:T(8,128)(2,1)}, u32[]{:S(2)}) copy-start(bf16[384,2048]{1,0:T(8,128)(2,1)} %param.9) | copy-start | bytes 4718596
Sparse Core Ops, SparseCore 0:
  29.7 30.8 reduce-scatter.2
  65.0 19.6 all-gather.2
  125.7 197.8 all-reduce.2
  348.3 27.1 reduce-scatter.4
  380.0 19.6 all-gather.4
where the time goes:
time: 425 us; the launch traced here: 424 us
  waiting for transfers between devices  272 us (64%)
  matrix products  71.1 us (17%)
  local copies, waits for them, and re-layouts  32.7 us (8%)
  other arithmetic  21.7 us (5%)
  between operations  13.4 us (3%)
  blocking collectives  12.1 us (3%)
    psum x1, waiting for transfers between devices, shards(): lax.psum(up_part.astype(jnp.bfloat16), 'request').astype(jnp.float32)  185 us
    reduce_scatter x1, waiting for transfers between devices, shards(): lax.psum_scatter(encode(product, signs[0], expos[0], 4).astype(jnp.float3...  28.2 us
    reduce_scatter x1, waiting for transfers between devices, shards(): lax.psum_scatter(encode(product, signs[2], expos[2], 4).astype(jnp.float3...  26.4 us
    all_gather x1, waiting for transfers between devices, shards(): final_rows = lax.all_gather(final_code, 'tensor', axis=0, tiled=True)  19.7 us
    dot_general x4, matrix products, unrotate(): jnp.dot(values.reshape(-1, 128), hadamard(), precision=lax.Precision.HIGH...  15.5 us
    dot_general x1, matrix products, shards(): product = jnp.dot(picked, down_weight, preferred_element_type=jnp.float32)  13.1 us
    all_gather x1, waiting for transfers between devices, shards(): gathered = lax.all_gather(coded, 'tensor', axis=0, tiled=True)  13.1 us
    dot_general x1, matrix products, shards(): up_part = jnp.dot(normed, up_weight, preferred_element_type=jnp.float32)  12.4 us
  transfers between devices with their start and end apart: 5, of which 5 were waited for; matrix products, arithmetic and copies ran while one was open for 2% of the time, Pallas kernels for 0%

commit v1 on v0

v1 whole, which is shorter than its diff:
```python
import functools

import jax
import jax.numpy as jnp
from jax import lax
from jax.experimental import pallas as pl
from jax.experimental.pallas import tpu as pltpu
from jax.sharding import PartitionSpec as P

D = 8192
MESH = pl.DeviceIdType.MESH
LAG = 2
VMEM_LIMIT = 52 * 2**20


def hadamard():
    index = jnp.arange(128, dtype=jnp.int32)
    common = jnp.bitwise_and(index[:, None], index[None, :])
    ones_count = jnp.zeros((128, 128), jnp.int32)
    for level in range(7):
        ones_count = ones_count + jnp.bitwise_and(jnp.right_shift(common, level), 1)
    return (1 - 2 * (ones_count % 2)).astype(jnp.bfloat16)


def turn(values, had):
    high = values.astype(jnp.bfloat16)
    low = (values - high.astype(jnp.float32)).astype(jnp.bfloat16)
    return jnp.dot(high, had, preferred_element_type=jnp.float32) + jnp.dot(low, had, preferred_element_type=jnp.float32)


def encode(values, sign, scale, had):
    return jnp.clip(turn(values * sign, had) * scale, -448.0, 448.0).astype(jnp.bfloat16)


def decode(codes, scale, had):
    return jnp.dot(codes, had, preferred_element_type=jnp.float32) * scale


def project_body(a_ref, w_ref, sign_ref, scale_ref, had_ref, o_ref):
    product = jnp.dot(a_ref[...], w_ref[...], preferred_element_type=jnp.float32)
    for low in range(0, product.shape[1], 128):
        cols = slice(low, low + 128)
        o_ref[:, cols] = encode(product[:, cols], sign_ref[:, cols], scale_ref[:, cols], had_ref[...])


def project(a, w, sign, scale, had):
    rows, depth = a.shape
    width = w.shape[1]
    block = 256
    return pl.pallas_call(
        project_body,
        grid=(width // block,),
        in_specs=[
            pl.BlockSpec((rows, depth), lambda j: (0, 0)),
            pl.BlockSpec((depth, block), lambda j: (0, j)),
            pl.BlockSpec((1, block), lambda j: (0, j)),
            pl.BlockSpec((1, block), lambda j: (0, j)),
            pl.BlockSpec((128, 128), lambda j: (0, 0)),
        ],
        out_specs=pl.BlockSpec((rows, block), lambda j: (0, j)),
        out_shape=jax.ShapeDtypeStruct((rows, width), jnp.bfloat16),
        compiler_params=pltpu.CompilerParams(vmem_limit_bytes=VMEM_LIMIT),
    )(a, w, sign, scale, had)


def recode_body(code_ref, base_ref, dec_ref, sign_ref, scale_ref, had_ref, state_ref, o_ref):
    for low in range(0, code_ref.shape[1], 128):
        cols = slice(low, low + 128)
        state = base_ref[:, cols].astype(jnp.float32) + decode(code_ref[:, cols], dec_ref[:, cols], had_ref[...])
        state_ref[:, cols] = state
        o_ref[:, cols] = encode(state, sign_ref[:, cols], scale_ref[:, cols], had_ref[...])


def recode(code, base, dec, sign, scale, had):
    return pl.pallas_call(
        recode_body,
        out_shape=(jax.ShapeDtypeStruct(code.shape, jnp.float32), jax.ShapeDtypeStruct(code.shape, jnp.bfloat16)),
        compiler_params=pltpu.CompilerParams(vmem_limit_bytes=VMEM_LIMIT),
    )(code, base, dec, sign, scale, had)


def finish_body(code_ref, dec_ref, had_ref, o_ref):
    for low in range(0, code_ref.shape[1], 128):
        cols = slice(low, low + 128)
        o_ref[:, cols] = decode(code_ref[:, cols], dec_ref[:, cols], had_ref[...]).astype(jnp.bfloat16)


def finish(code, dec, had):
    rows, width = code.shape
    block = min(width, 512)
    return pl.pallas_call(
        finish_body,
        grid=(width // block,),
        in_specs=[
            pl.BlockSpec((rows, block), lambda j: (0, j)),
            pl.BlockSpec((1, block), lambda j: (0, j)),
            pl.BlockSpec((128, 128), lambda j: (0, 0)),
        ],
        out_specs=pl.BlockSpec((rows, block), lambda j: (0, j)),
        out_shape=jax.ShapeDtypeStruct((rows, width), jnp.bfloat16),
        compiler_params=pltpu.CompilerParams(vmem_limit_bytes=VMEM_LIMIT),
    )(code, dec, had)


def ffn_body(n, chunks, cw, code_ref, dec_ref, gain_ref, had_ref, gate_ref, up_ref, h_ref,
             x_ref, sq_ref, sqr_ref, w_ref, p_ref, r_ref,
             w_sem, rs_send, rs_recv, ag_send, ag_recv, sq_send, sq_recv):
    z = lax.axis_index("request")
    half = p_ref.shape[2]

    def weights(c, slot):
        cols = pl.ds(pl.multiple_of(c * cw, cw), cw)
        return (
            pltpu.make_async_copy(gate_ref.at[:, cols], w_ref.at[slot, :, pl.ds(0, cw)], w_sem.at[slot, 0]),
            pltpu.make_async_copy(up_ref.at[:, cols], w_ref.at[slot, :, pl.ds(cw, cw)], w_sem.at[slot, 1]),
        )

    barrier = pltpu.get_barrier_semaphore()

    @pl.when(z > 0)
    def _():
        pl.semaphore_signal(barrier, inc=1, device_id={"request": z - 1}, device_id_type=MESH)

    @pl.when(z < n - 1)
    def _():
        pl.semaphore_signal(barrier, inc=1, device_id={"request": z + 1}, device_id_type=MESH)

    for copy in weights(0, 0):
        copy.start()

    sq_ref[...] = jnp.zeros_like(sq_ref)

    @pl.loop(0, code_ref.shape[1] // 128)
    def _(b):
        cols = pl.ds(pl.multiple_of(b * 128, 128), 128)
        restored = decode(code_ref[:, cols], dec_ref[:, cols], had_ref[...])
        squared = restored * restored
        sq_ref[0] += squared[:half]
        sq_ref[1] += squared[half:]
        x_ref[:, cols] = (restored * gain_ref[:, cols]).astype(jnp.bfloat16)

    pl.semaphore_wait(barrier, (z > 0).astype(jnp.int32) + (z < n - 1).astype(jnp.int32))

    place = (n - 1 - z, z)
    after = (z - 1, z + 1)
    before = (z + 1, z - 1)

    def sum_copy(d, c):
        return pltpu.make_async_remote_copy(
            src_ref=p_ref.at[d, c], dst_ref=r_ref.at[d, c], send_sem=rs_send.at[d, c], recv_sem=rs_recv.at[d, c],
            device_id={"request": after[d]}, device_id_type=MESH)

    def square_copy(d):
        return pltpu.make_async_remote_copy(
            src_ref=sq_ref.at[d], dst_ref=sqr_ref.at[d], send_sem=sq_send.at[d], recv_sem=sq_recv.at[d],
            device_id={"request": after[d]}, device_id_type=MESH)

    def hidden_copy(d, c):
        part = h_ref.at[pl.ds(d * half, half), pl.ds(pl.multiple_of(c * cw, cw), cw)]
        return pltpu.make_async_remote_copy(
            src_ref=part, dst_ref=part, send_sem=ag_send.at[d, c], recv_sem=ag_recv.at[d, c],
            device_id={"request": before[d]}, device_id_type=MESH)

    @pl.loop(0, chunks + 2 * (n - 1) * LAG)
    def _(s):
        @pl.when(s < chunks)
        def _():
            slot = lax.rem(s, 2)

            @pl.when(s + 1 < chunks)
            def _():
                for copy in weights(s + 1, 1 - slot):
                    copy.start()

            for copy in weights(s, slot):
                copy.wait()
            total = jnp.dot(x_ref[...], w_ref[slot], preferred_element_type=jnp.float32).astype(jnp.bfloat16)
            p_ref[0, s] = total[:half]
            p_ref[1, s] = total[half:]

        for d in (0, 1):
            pos = place[d]
            c = s - pos * LAG

            @pl.when((c >= 0) & (c < chunks))
            def _(d=d, pos=pos, c=c):
                @pl.when(c == 0)
                def _():
                    @pl.when(pos > 0)
                    def _():
                        square_copy(d).wait_recv()
                        sq_ref[d] += sqr_ref[d]

                    @pl.when(pos < n - 1)
                    def _():
                        square_copy(d).start()

                    @pl.when(pos == n - 1)
                    def _():
                        total = jnp.sum(sq_ref[d], axis=1, keepdims=True)
                        sq_ref[d] = jnp.broadcast_to(lax.rsqrt(total / D + 1e-05), sq_ref.shape[1:])

                @pl.when(pos > 0)
                def _():
                    sum_copy(d, c).wait_recv()
                    p_ref[d, c] = (p_ref[d, c].astype(jnp.float32) + r_ref[d, c].astype(jnp.float32)).astype(jnp.bfloat16)

                @pl.when(pos < n - 1)
                def _():
                    sum_copy(d, c).start()

                @pl.when(pos == n - 1)
                def _():
                    cols = pl.multiple_of(c * cw, cw)
                    for low in range(0, cw, 128):
                        factor = sq_ref[d]
                        gate = p_ref[d, c, :, low:low + 128].astype(jnp.float32) * factor
                        up = p_ref[d, c, :, cw + low:cw + low + 128].astype(jnp.float32) * factor
                        value = gate / (1.0 + jnp.exp(-gate)) * up
                        h_ref[pl.ds(d * half, half), pl.ds(pl.multiple_of(cols + low, 128), 128)] = value.astype(jnp.bfloat16)
                    hidden_copy(d, c).start()

            back = s - (2 * (n - 1) - pos) * LAG

            @pl.when((pos < n - 1) & (back >= 0) & (back < chunks))
            def _(d=d, pos=pos, back=back):
                hidden_copy(d, back).wait_recv()

                @pl.when(pos > 0)
                def _():
                    hidden_copy(d, back).start()

    for d in (0, 1):
        pos = place[d]

        @pl.when(pos < n - 1)
        def _(d=d):
            square_copy(d).wait_send()

            @pl.loop(0, chunks)
            def _(c):
                sum_copy(d, c).wait_send()

        @pl.when(pos > 0)
        def _(d=d):
            @pl.loop(0, chunks)
            def _(c):
                hidden_copy(d, c).wait_send()


def ffn(n, code, dec, gain, had, gate_weight, up_weight):
    rows, depth = code.shape
    units = gate_weight.shape[1]
    cw = 128
    chunks = units // cw
    half = rows // 2
    vmem = pl.BlockSpec(memory_space=pltpu.VMEM)
    return pl.pallas_call(
        functools.partial(ffn_body, n, chunks, cw),
        out_shape=jax.ShapeDtypeStruct((rows, units), jnp.bfloat16),
        in_specs=[vmem] * 4 + [pl.BlockSpec(memory_space=pl.ANY)] * 2,
        out_specs=vmem,
        scratch_shapes=[
            pltpu.VMEM((rows, depth), jnp.bfloat16),
            pltpu.VMEM((2, half, 128), jnp.float32),
            pltpu.VMEM((2, half, 128), jnp.float32),
            pltpu.VMEM((2, depth, 2 * cw), jnp.bfloat16),
            pltpu.VMEM((2, chunks, half, 2 * cw), jnp.bfloat16),
            pltpu.VMEM((2, chunks, half, 2 * cw), jnp.bfloat16),
            pltpu.SemaphoreType.DMA((2, 2)),
            pltpu.SemaphoreType.DMA((2, chunks)),
            pltpu.SemaphoreType.DMA((2, chunks)),
            pltpu.SemaphoreType.DMA((2, chunks)),
            pltpu.SemaphoreType.DMA((2, chunks)),
            pltpu.SemaphoreType.DMA((2,)),
            pltpu.SemaphoreType.DMA((2,)),
        ],
        compiler_params=pltpu.CompilerParams(collective_id=0, has_side_effects=True, vmem_limit_bytes=VMEM_LIMIT),
    )(code, dec, gain, had, gate_weight, up_weight)


def shards(n_request, attn_heads, out_weight, resid, gain, gate_weight, up_weight, down_weight, signs, expos):
    had = hadamard()
    sign = (2 * signs - 1).astype(jnp.float32)
    shift = expos + jnp.array([[4], [8], [4], [6]], jnp.int32)
    enc = jnp.repeat(0.125 * jnp.exp2(-shift.astype(jnp.float32)), 128, axis=1)
    dec = jnp.repeat(0.0625 * jnp.exp2(shift.astype(jnp.float32)), 128, axis=1) * sign
    row = lambda table, k: table[k:k + 1]

    coded = project(attn_heads, out_weight, row(sign, 0), row(enc, 0), had)
    summed = lax.psum_scatter(coded, "tensor", scatter_dimension=0, tiled=True)
    hidden_state, coded = recode(summed, resid, row(dec, 0), row(sign, 1), row(enc, 1), had)
    gathered = lax.all_gather(coded, "tensor", axis=0, tiled=True)
    hidden = ffn(n_request, gathered, row(dec, 1), gain.astype(jnp.float32)[None, :], had, gate_weight, up_weight)
    coded = project(hidden, down_weight, row(sign, 2), row(enc, 2), had)
    summed = lax.psum_scatter(coded, "tensor", scatter_dimension=0, tiled=True)
    _, coded = recode(summed, hidden_state, row(dec, 2), row(sign, 3), row(enc, 3), had)
    gathered = lax.all_gather(coded, "tensor", axis=0, tiled=True)
    return finish(gathered, row(dec, 3), had)


def solution(mesh):
    return jax.shard_map(
        functools.partial(shards, mesh.shape["request"]),
        mesh=mesh,
        in_specs=(
            P("parts", "tensor"),
            P("tensor", "request"),
            P(("parts", "tensor"), "request"),
            P("request"),
            P("request", "tensor"),
            P("request", "tensor"),
            P("tensor", "request"),
            P(None, "request"),
            P(None, "request"),
        ),
        out_specs=P("parts", "request"),
        check_vma=False,
    )
```

time: 425 us -> 269 us (0.63)
  waiting for transfers between devices: 272 us -> 95.4 us
  Pallas kernels: 0 us -> 151 us
  matrix products: 71.1 us -> 0 us
  local copies, waits for them, and re-layouts: 32.7 us -> 6.73 us
  other arithmetic: 21.7 us -> 1.65 us
  blocking collectives: 12.1 us -> 0 us
    psum x1 -> x0, waiting for transfers between devices: 185 us -> none  [shards(): lax.psum(up_part.astype(jnp.bfloat16), 'request').astype(jnp.float32)]
    pallas_call x0 -> x6, Pallas kernels: none -> 151 us  [the longest x1 117 us: ffn(): pl.pallas_call(functools.partial(ffn_body, n, chunks, cw), out_shape=jax....]
    dot_general x12 -> x0, matrix products: 71.1 us -> none  [the longest x4 15.5 us: unrotate(): jnp.dot(values.reshape(-1, 128), hadamard(), precision=lax.Precision.HIGH...]
    all_gather x1 -> x2, waiting for transfers between devices: 13.1 us -> 39.5 us  [shards(): gathered = lax.all_gather(coded, 'tensor', axis=0, tiled=True)]
    reshape x16 -> x0, local copies, waits for them, and re-layouts: 23.9 us -> none  [the longest x4 7.25 us: unrotate(): turned.reshape(shape) * 0.0625 * (2 * sign_bits - 1).astype(jnp.float32)]
    all_gather x1 -> x0, waiting for transfers between devices: 19.7 us -> none  [shards(): final_rows = lax.all_gather(final_code, 'tensor', axis=0, tiled=True)]
    psum x1 -> x0, blocking collectives: 12.1 us -> none  [shards(): lax.psum(squares.astype(jnp.bfloat16), 'request').astype(jnp.float32)]
    convert_element_type x7 -> x2, other arithmetic: 10.8 us -> 0.86 us  [the longest x1 0.77 us: shards(): sign = (2 * signs - 1).astype(jnp.float32)]
  transfers between devices with their start and end apart: 5 -> 4, of which waited for: 5 -> 4; matrix products, arithmetic and copies ran while one was open for 2% -> 0% of each run, Pallas kernels for 0% -> 0%
where the time goes in v1:
time: 269 us; the launch traced here: 268 us
  Pallas kernels  151 us (56%)
  waiting for transfers between devices  95.4 us (35%)
  between operations  13.2 us (5%)
  local copies, waits for them, and re-layouts  6.73 us (3%)
    pallas_call x1, Pallas kernels, ffn(): pl.pallas_call(functools.partial(ffn_body, n, chunks, cw), out_shape=jax....  117 us
    reduce_scatter x2, waiting for transfers between devices, shards(): summed = lax.psum_scatter(coded, 'tensor', scatter_dimension=0, tiled=True)  55.8 us
    all_gather x2, waiting for transfers between devices, shards(): gathered = lax.all_gather(coded, 'tensor', axis=0, tiled=True)  39.5 us
    pallas_call x2, Pallas kernels, project(): pl.pallas_call(project_body, grid=(width // block,), in_specs=[pl.BlockSp...  25.6 us
    unnamed x17, local copies, waits for them, and re-layouts  6.39 us
    pallas_call x2, Pallas kernels, recode(): pl.pallas_call(recode_body, out_shape=(jax.ShapeDtypeStruct(code.shape, j...  5.89 us
  transfers between devices with their start and end apart: 4, of which 4 were waited for; matrix products, arithmetic and copies ran while one was open for 0% of the time, Pallas kernels for 0%

profile of v1, /device:TPU:0, one launch (start us, length us, event | category | flops | bytes accessed | tf_op | source)
XLA Modules:
  0.0 268.1 jit_solution(8294058911564736393)
XLA Ops:
  6.5 0.1 fusion.3.had_ref
  6.6 0.8 exponential_multiply_fusion
  7.4 0.8 add_convert_fusion
  8.2 0.1 broadcast_in_dim.27
  8.3 11.3 %shard_map.100 = bf16[384,2048]{1,0:T(8,128)(2,1)} custom-call(bf16[384,2048]{1,0:T(8,128)(2,1)} %a_ref.1, bf16[2048,2048]{1,0:T(8,128)(2,1)} %w_ref.2, f32[1,2048]{1,0:T(1,128)S(1)} %get-tuple-element.18.sign_ref, f32[1,2048]{1,0:T(1,128)S(1)} %bitcast.21, bf16[128,128]{1,0:T(8,128)(2,1)S(1)} %fusion.3.had_ref), custom_call_target="tpu_custom_call" | custom-call | tf_op jit(solution)/shard_map/pallas_call | solution.py:50
  19.7 0.1 broadcast_bitcast_fusion
  19.8 0.6 copy-done.6
  20.4 30.2 %reduce-scatter.3.cloned.1.call-done.code_ref = bf16[96,2048]{1,0:T(8,128)(2,1)} async-done(((bf16[384,2048]{1,0:T(8,128)(2,1)}), bf16[96,2048]{1,0:T(8,128)(2,1)}) %reduce-scatter.3.cloned.1.call-update) | async-done | bytes 393232 | tf_op jit(solution)/shard_map/reduce_scatter | solution.py:291
  50.7 0.1 broadcast_in_dim.30
  50.8 1.0 copy-done.4
  51.8 2.3 shard_map.101
  54.1 0.9 copy-done.2
  55.1 19.7 %all-gather.3.cloned.1.call-done.code_ref = bf16[384,2048]{1,0:T(8,128)(2,1)} async-done(((bf16[96,2048]{1,0:T(8,128)(2,1)}), bf16[384,2048]{1,0:T(8,128)(2,1)}) %all-gather.3.cloned.1.call-update) | async-done | bytes 1572880 | tf_op jit(solution)/shard_map/all_gather | solution.py:293
  74.8 1.4 copy-done
  76.2 117.2 %shard_map.102.a_ref = bf16[384,3584]{1,0:T(8,128)(2,1)} custom-call(bf16[384,2048]{1,0:T(8,128)(2,1)S(1)} %copy-done, f32[1,2048]{1,0:T(1,128)S(1)} %get-tuple-element.13.dec_ref, f32[1,2048]{1,0:T(1,128)S(1)} %bitcast.19, bf16[128,128]{1,0:T(8,128)(2,1)S(1)} %fusion.3.had_ref, bf16[2048,3584]{1,0:T(8,128)(2,1)} %gate_ref.1, bf16[2048,3584]{1,0:T(8,128)(2,1)} %up_ref.1), custom_call_target="tpu_custom_call" | custom-call | tf_op jit(solution)/shard_map/pallas_call | solution.py:258
  193.4 0.1 broadcast_in_dim.34
  193.5 14.3 %shard_map.103 = bf16[384,2048]{1,0:T(8,128)(2,1)} custom-call(bf16[384,3584]{1,0:T(8,128)(2,1)} %shard_map.102.a_ref, bf16[3584,2048]{1,0:T(8,128)(2,1)} %w_ref.3, f32[1,2048]{1,0:T(1,128)S(1)} %get-tuple-element.16.sign_ref, f32[1,2048]{1,0:T(1,128)S(1)} %bitcast.20, bf16[128,128]{1,0:T(8,128)(2,1)S(1)} %fusion.3.had_ref), custom_call_target="tpu_custom_call" | custom-call | tf_op jit(solution)/shard_map/pallas_call | solution.py:50
  207.8 25.5 %reduce-scatter.5.cloned.1.call-done.code_ref = bf16[96,2048]{1,0:T(8,128)(2,1)} async-done(((bf16[384,2048]{1,0:T(8,128)(2,1)}), bf16[96,2048]{1,0:T(8,128)(2,1)}) %reduce-scatter.5.cloned.1.call-update) | async-done | bytes 393232 | tf_op jit(solution)/shard_map/reduce_scatter | solution.py:296
  233.4 0.1 broadcast_in_dim.36
  233.4 1.0 copy-done.5
  234.4 3.6 %shard_map.104 = (f32[96,2048]{1,0:T(8,128)}, bf16[96,2048]{1,0:T(8,128)(2,1)}) custom-call(bf16[96,2048]{1,0:T(8,128)(2,1)S(1)} %copy-done.5, f32[96,2048]{1,0:T(8,128)} %copy-done.2, f32[1,2048]{1,0:T(1,128)S(1)} %get-tuple-element.12.dec_ref, f32[1,2048]{1,0:T(1,128)S(1)} %get-tuple-element.15.sign_ref, f32[1,2048]{1,0:T(1,128)S(1)} %bitcast.17, ...), custom_call_target="tpu_custom_call" | custom-call | tf_op jit(solution)/shard_map/pallas_call | solution.py:75
  238.0 19.8 %all-gather.5.cloned.1.call-done.code_ref = bf16[384,2048]{1,0:T(8,128)(2,1)} async-done(((bf16[96,2048]{1,0:T(8,128)(2,1)}), bf16[384,2048]{1,0:T(8,128)(2,1)}) %all-gather.5.cloned.1.call-update) | async-done | bytes 1572880 | tf_op jit(solution)/shard_map/all_gather | solution.py:298
  257.8 1.4 copy-done.1
  259.3 2.3 shard_map.105
  (23 shorter events, 0.3 us)
Async XLA Ops:
  6.5 44.1 %reduce-scatter.3.cloned.1.call-start = ((), (), s32[]{:S(2)}) async-start(), calls=%async_computation.2 | async-start | bytes 1966080 | tf_op jit(solution)/shard_map/reduce_scatter | solution.py:291
  19.6 0.8 copy-start.6
  19.6 31.1 %copy-start.3 = (bf16[96,2048]{1,0:T(8,128)(2,1)S(1)}, bf16[96,2048]{1,0:T(8,128)(2,1)}, u32[]{:S(2)}) copy-start(bf16[96,2048]{1,0:T(8,128)(2,1)} %base_ref.1) | copy-start | bytes 1179652
  19.6 35.4 %copy-start.7 = (bf16[2048]{0:T(1024)(128)(2,1)S(1)}, bf16[2048]{0:T(1024)(128)(2,1)}, u32[]{:S(2)}) copy-start(bf16[2048]{0:T(1024)(128)(2,1)} %param.13) | copy-start | bytes 12292
  19.7 55.1 %all-gather.3.cloned.1.call-start = ((), (), s32[]{:S(2)}) async-start(), calls=%async_computation.3 | async-start | bytes 1966080 | tf_op jit(solution)/shard_map/all_gather | solution.py:293
  50.8 1.0 copy-start.4
  54.1 0.9 copy-start.2
  55.0 178.4 %reduce-scatter.5.cloned.1.call-start = ((), (), s32[]{:S(2)}) async-start(), calls=%async_computation.4 | async-start | bytes 1966080 | tf_op jit(solution)/shard_map/reduce_scatter | solution.py:296
  74.8 1.4 copy-start
  207.8 50.1 %all-gather.5.cloned.1.call-start = ((), (), s32[]{:S(2)}) async-start(), calls=%async_computation.5 | async-start | bytes 1966080 | tf_op jit(solution)/shard_map/all_gather | solution.py:298
  233.4 1.0 copy-start.5
  257.8 1.4 copy-start.1
Sparse Core Ops, SparseCore 0:
  19.8 30.8 reduce-scatter.2
  55.1 19.6 all-gather.2
  207.9 25.4 reduce-scatter.4
  238.2 19.6 all-gather.4

commit v2 on v1

--- a/solution.py
+++ b/solution.py
@@ -63,20 +63,118 @@
     )(a, w, sign, scale, had)
 
 
-def recode_body(code_ref, base_ref, dec_ref, sign_ref, scale_ref, had_ref, state_ref, o_ref):
-    for low in range(0, code_ref.shape[1], 128):
-        cols = slice(low, low + 128)
-        state = base_ref[:, cols].astype(jnp.float32) + decode(code_ref[:, cols], dec_ref[:, cols], had_ref[...])
-        state_ref[:, cols] = state
-        o_ref[:, cols] = encode(state, sign_ref[:, cols], scale_ref[:, cols], had_ref[...])
-
-
-def recode(code, base, dec, sign, scale, had):
-    return pl.pallas_call(
-        recode_body,
-        out_shape=(jax.ShapeDtypeStruct(code.shape, jnp.float32), jax.ShapeDtypeStruct(code.shape, jnp.bfloat16)),
-        compiler_params=pltpu.CompilerParams(vmem_limit_bytes=VMEM_LIMIT),
-    )(code, base, dec, sign, scale, had)
+def exchange_body(nx, parts, keep, code_ref, base_ref, dec_ref, sign_ref, scale_ref, had_ref, *refs):
+    if keep:
+        state_ref, *refs = refs
+    (o_ref, s_ref, q_ref, g_ref, pair_send, pair_recv, sum_send, sum_recv, out_send, out_recv, fwd_send, fwd_recv) = refs
+    t = lax.axis_index("tensor")
+    core = lax.rem(t, 2)
+    chip = t // 2
+    width = code_ref.shape[3] // parts
+    sibling = chip * 2 + 1 - core
+
+    def chip_at(k):
+        return lax.rem(chip + k + nx, nx)
+
+    def span(j):
+        return slice(j * width, (j + 1) * width)
+
+    def cols(j):
+        return pl.ds(j * width, width)
+
+    def pair_copy(j):
+        return pltpu.make_async_remote_copy(
+            src_ref=code_ref.at[:, 1 - core, :, cols(j)], dst_ref=s_ref.at[:, :, cols(j)],
+            send_sem=pair_send.at[j], recv_sem=pair_recv.at[j],
+            device_id={"tensor": sibling}, device_id_type=MESH)
+
+    def sum_copy(k, j):
+        return pltpu.make_async_remote_copy(
+            src_ref=q_ref.at[chip_at(k), :, cols(j)], dst_ref=g_ref.at[k - 1, :, cols(j)],
+            send_sem=sum_send.at[k - 1, j], recv_sem=sum_recv.at[k - 1, j],
+            device_id={"tensor": chip_at(k) * 2 + core}, device_id_type=MESH)
+
+    def out_copy(k, j):
+        part = o_ref.at[chip, core, :, cols(j)]
+        return pltpu.make_async_remote_copy(
+            src_ref=part, dst_ref=part, send_sem=out_send.at[k - 1, j], recv_sem=out_recv.at[k - 1, j],
+            device_id={"tensor": chip_at(k) * 2 + core}, device_id_type=MESH)
+
+    def forward_copy(k, j):
+        part = o_ref.at[chip_at(-k), core, :, cols(j)]
+        return pltpu.make_async_remote_copy(
+            src_ref=part, dst_ref=part, send_sem=fwd_send.at[k, j], recv_sem=fwd_recv.at[k, j],
+            device_id={"tensor": sibling}, device_id_type=MESH)
+
+    barrier = pltpu.get_barrier_semaphore()
+    pl.semaphore_signal(barrier, inc=1, device_id={"tensor": sibling}, device_id_type=MESH)
+    for k in range(1, nx):
+        pl.semaphore_signal(barrier, inc=1, device_id={"tensor": chip_at(k) * 2 + core}, device_id_type=MESH)
+    pl.semaphore_wait(barrier, nx)
+
+    for j in range(parts):
+        pair_copy(j).start()
+    for j in range(parts):
+        pair_copy(j).wait_recv()
+        for chip_to in range(nx):
+            both = code_ref[chip_to, core, :, span(j)].astype(jnp.float32) + s_ref[chip_to, :, span(j)].astype(jnp.float32)
+            q_ref[chip_to, :, span(j)] = both.astype(jnp.bfloat16)
+        for k in range(1, nx):
+            sum_copy(k, j).start()
+    for j in range(parts):
+        total = q_ref[chip, :, span(j)].astype(jnp.float32)
+        for k in range(1, nx):
+            sum_copy(k, j).wait_recv()
+            total += g_ref[k - 1, :, span(j)].astype(jnp.float32)
+        total = total.astype(jnp.bfloat16)
+        for low in range(0, width, 128):
+            here = slice(j * width + low, j * width + low + 128)
+            state = base_ref[:, here].astype(jnp.float32) + decode(total[:, low:low + 128], dec_ref[:, here], had_ref[...])
+            if keep:
+                state_ref[:, here] = state
+            o_ref[chip, core, :, here] = encode(state, sign_ref[:, here], scale_ref[:, here], had_ref[...])
+        for k in range(1, nx):
+            out_copy(k, j).start()
+        forward_copy(0, j).start()
+    for j in range(parts):
+        for k in range(1, nx):
+            out_copy(k, j).wait_recv()
+            forward_copy(k, j).start()
+    for j in range(parts):
+        pair_copy(j).wait_send()
+        for k in range(nx):
+            forward_copy(k, j).wait()
+        for k in range(1, nx):
+            sum_copy(k, j).wait_send()
+            out_copy(k, j).wait_send()
+
+
+def exchange(n_tensor, keep, name, code, base, dec, sign, scale, had):
+    rows, width = code.shape
+    nx, own, parts = n_tensor // 2, rows // n_tensor, 4
+    vmem = pl.BlockSpec(memory_space=pltpu.VMEM)
+    states = [jax.ShapeDtypeStruct((own, width), jnp.float32)] if keep else []
+    *state, out = pl.pallas_call(
+        functools.partial(exchange_body, nx, parts, keep),
+        out_shape=states + [jax.ShapeDtypeStruct((nx, 2, own, width), jnp.bfloat16)],
+        in_specs=[vmem] * 6,
+        out_specs=[vmem] * (len(states) + 1),
+        scratch_shapes=[
+            pltpu.VMEM((nx, own, width), jnp.bfloat16),
+            pltpu.VMEM((nx, own, width), jnp.bfloat16),
+            pltpu.VMEM((nx - 1, own, width), jnp.bfloat16),
+            pltpu.SemaphoreType.DMA((parts,)),
+            pltpu.SemaphoreType.DMA((parts,)),
+            pltpu.SemaphoreType.DMA((nx - 1, parts)),
+            pltpu.SemaphoreType.DMA((nx - 1, parts)),
+            pltpu.SemaphoreType.DMA((nx - 1, parts)),
+            pltpu.SemaphoreType.DMA((nx - 1, parts)),
+            pltpu.SemaphoreType.DMA((nx, parts)),
+            pltpu.SemaphoreType.DMA((nx, parts)),
+        ],
+        compiler_params=pltpu.CompilerParams(collective_id=name, has_side_effects=True, vmem_limit_bytes=VMEM_LIMIT),
+    )(code.reshape(nx, 2, own, width), base, dec, sign, scale, had)
+    return (*state, out.reshape(rows, width))
 
 
 def finish_body(code_ref, dec_ref, had_ref, o_ref):
@@ -279,7 +377,7 @@
     )(code, dec, gain, had, gate_weight, up_weight)
 
 
-def shards(n_request, attn_heads, out_weight, resid, gain, gate_weight, up_weight, down_weight, signs, expos):
+def shards(n_tensor, n_request, attn_heads, out_weight, resid, gain, gate_weight, up_weight, down_weight, signs, expos):
     had = hadamard()
     sign = (2 * signs - 1).astype(jnp.float32)
     shift = expos + jnp.array([[4], [8], [4], [6]], jnp.int32)
@@ -288,20 +386,16 @@
     row = lambda table, k: table[k:k + 1]
 
     coded = project(attn_heads, out_weight, row(sign, 0), row(enc, 0), had)
-    summed = lax.psum_scatter(coded, "tensor", scatter_dimension=0, tiled=True)
-    hidden_state, coded = recode(summed, resid, row(dec, 0), row(sign, 1), row(enc, 1), had)
-    gathered = lax.all_gather(coded, "tensor", axis=0, tiled=True)
+    hidden_state, gathered = exchange(n_tensor, True, 1, coded, resid, row(dec, 0), row(sign, 1), row(enc, 1), had)
     hidden = ffn(n_request, gathered, row(dec, 1), gain.astype(jnp.float32)[None, :], had, gate_weight, up_weight)
     coded = project(hidden, down_weight, row(sign, 2), row(enc, 2), had)
-    summed = lax.psum_scatter(coded, "tensor", scatter_dimension=0, tiled=True)
-    _, coded = recode(summed, hidden_state, row(dec, 2), row(sign, 3), row(enc, 3), had)
-    gathered = lax.all_gather(coded, "tensor", axis=0, tiled=True)
+    (gathered,) = exchange(n_tensor, False, 2, coded, hidden_state, row(dec, 2), row(sign, 3), row(enc, 3), had)
     return finish(gathered, row(dec, 3), had)
 
 
 def solution(mesh):
     return jax.shard_map(
-        functools.partial(shards, mesh.shape["request"]),
+        functools.partial(shards, mesh.shape["tensor"], mesh.shape["request"]),
         mesh=mesh,
         in_specs=(
             P("parts", "tensor"),

time: 269 us -> 204 us (0.76)
  waiting for transfers between devices: 95.4 us -> 0 us
  Pallas kernels: 151 us -> 195 us
  between operations: 13.2 us -> 0.12 us
    reduce_scatter x2 -> x0, waiting for transfers between devices: 55.8 us -> none  [shards(): summed = lax.psum_scatter(coded, 'tensor', scatter_dimension=0, tiled=True)]
    pallas_call x2, Pallas kernels: 5.89 us -> 50.4 us  [exchange(): pl.pallas_call(functools.partial(exchange_body, nx, parts, keep), out_sha...]
    all_gather x2 -> x0, waiting for transfers between devices: 39.5 us -> none  [shards(): gathered = lax.all_gather(coded, 'tensor', axis=0, tiled=True)]
    unnamed x17 -> x13, local copies, waits for them, and re-layouts: 6.39 us -> 5.16 us
  transfers between devices with their start and end apart: 4 -> 0, of which waited for: 4 -> 0; matrix products, arithmetic and copies ran while one was open for 0% -> 0% of each run, Pallas kernels for 0% -> 0%
where the time goes in v2:
time: 204 us; the launch traced here: 203 us
  Pallas kernels  195 us (96%)
  local copies, waits for them, and re-layouts  5.49 us (3%)
  other arithmetic  2.41 us (1%)
    pallas_call x1, Pallas kernels, ffn(): pl.pallas_call(functools.partial(ffn_body, n, chunks, cw), out_shape=jax....  118 us
    pallas_call x2, Pallas kernels, exchange(): pl.pallas_call(functools.partial(exchange_body, nx, parts, keep), out_sha...  50.4 us
    pallas_call x2, Pallas kernels, project(): pl.pallas_call(project_body, grid=(width // block,), in_specs=[pl.BlockSp...  23.9 us
    unnamed x13, local copies, waits for them, and re-layouts  5.16 us

profile of v2, /device:TPU:0, one launch (start us, length us, event | category | flops | bytes accessed | tf_op | source)
XLA Modules:
  0.0 202.7 jit_solution(16456307092290637806)
XLA Ops:
  0.0 0.8 exponential_multiply_fusion
  0.8 0.1 broadcast_bitcast_fusion
  0.8 0.8 bitcast_multiply_fusion
  1.6 0.8 add_convert_fusion
  2.5 0.1 fusion.3.had_ref
  2.6 0.1 broadcast_in_dim.27
  2.6 10.5 %shard_map.100 = bf16[384,2048]{1,0:T(8,128)(2,1)S(1)} custom-call(bf16[384,2048]{1,0:T(8,128)(2,1)} %a_ref.1, bf16[2048,2048]{1,0:T(8,128)(2,1)} %w_ref.2, f32[1,2048]{1,0:T(1,128)S(1)} %get-tuple-element.23.sign_ref, f32[1,2048]{1,0:T(1,128)S(1)} %bitcast.29, bf16[128,128]{1,0:T(8,128)(2,1)S(1)} %fusion.3.had_ref), custom_call_target="tpu_custom_call" | custom-call | tf_op jit(solution)/shard_map/pallas_call | solution.py:50
  13.1 0.0 copy-start.1
  13.1 1.1 copy-done.1
  14.3 0.1 broadcast_in_dim.30
  14.4 0.0 copy-done.4
  14.4 26.0 %shard_map.101 = (f32[96,2048]{1,0:T(8,128)S(1)}, bf16[2,2,96,2048]{3,2,1,0:T(8,128)(2,1)}) custom-call(bf16[2,2,96,2048]{3,2,1,0:T(8,128)(2,1)} %bitcast.22, bf16[96,2048]{1,0:T(8,128)(2,1)S(1)} %copy-done.4, f32[1,2048]{1,0:T(1,128)S(1)} %get-tuple-element.12.dec_ref, f32[1,2048]{1,0:T(1,128)S(1)} %get-tuple-element.24.sign_ref, f32[1,2048]{1,0:T(1,128)S(1)} %bitcast.25, ...), custom_call_target="tpu_custom_call" | custom-call | tf_op jit(solution)/shard_map/pallas_call | solution.py:157
  40.4 0.0 copy-done.5
  40.4 0.0 copy-start.3
  40.4 1.4 copy-done.3
  41.8 118.1 %shard_map.102.a_ref = bf16[384,3584]{1,0:T(8,128)(2,1)} custom-call(bf16[384,2048]{1,0:T(8,128)(2,1)S(1)} %bitcast.24, f32[1,2048]{1,0:T(1,128)S(1)} %get-tuple-element.11.dec_ref, f32[1,2048]{1,0:T(1,128)S(1)} %bitcast.28, bf16[128,128]{1,0:T(8,128)(2,1)S(1)} %fusion.3.had_ref, bf16[2048,3584]{1,0:T(8,128)(2,1)} %gate_ref.1, bf16[2048,3584]{1,0:T(8,128)(2,1)} %up_ref.1), custom_call_target="tpu_custom_call" | custom-call | tf_op jit(solution)/shard_map/pallas_call | solution.py:356
  159.9 0.1 broadcast_in_dim.34
  160.0 13.4 %shard_map.103 = bf16[384,2048]{1,0:T(8,128)(2,1)S(1)} custom-call(bf16[384,3584]{1,0:T(8,128)(2,1)} %shard_map.102.a_ref, bf16[3584,2048]{1,0:T(8,128)(2,1)} %w_ref.3, f32[1,2048]{1,0:T(1,128)S(1)} %get-tuple-element.25.sign_ref, f32[1,2048]{1,0:T(1,128)S(1)} %bitcast.27, bf16[128,128]{1,0:T(8,128)(2,1)S(1)} %fusion.3.had_ref), custom_call_target="tpu_custom_call" | custom-call | tf_op jit(solution)/shard_map/pallas_call | solution.py:50
  173.3 0.0 copy-start.2
  173.4 1.1 copy-done.2
  174.5 0.1 broadcast_in_dim.36
  174.6 24.4 %shard_map.104 = bf16[2,2,96,2048]{3,2,1,0:T(8,128)(2,1)} custom-call(bf16[2,2,96,2048]{3,2,1,0:T(8,128)(2,1)} %bitcast.23, f32[96,2048]{1,0:T(8,128)S(1)} %get-tuple-element.8.base_ref, f32[1,2048]{1,0:T(1,128)S(1)} %get-tuple-element.10.dec_ref, f32[1,2048]{1,0:T(1,128)S(1)} %get-tuple-element.26.sign_ref, f32[1,2048]{1,0:T(1,128)S(1)} %bitcast.26, ...), custom_call_target="tpu_custom_call" | custom-call | tf_op jit(solution)/shard_map/pallas_call | solution.py:157
  199.0 1.4 copy-done
  200.4 2.3 %shard_map.105 = bf16[384,2048]{1,0:T(8,128)(2,1)} custom-call(bf16[384,2048]{1,0:T(8,128)(2,1)S(1)} %bitcast.21, f32[1,2048]{1,0:T(1,128)S(1)} %get-tuple-element.9.dec_ref, bf16[128,128]{1,0:T(8,128)(2,1)S(1)} %fusion.3.had_ref), custom_call_target="tpu_custom_call" | custom-call | tf_op jit(solution)/shard_map/pallas_call | solution.py:189
  (6 shorter events, 0.1 us)
Async XLA Ops:
  2.6 11.7 %copy-start.4 = (bf16[96,2048]{1,0:T(8,128)(2,1)S(1)}, bf16[96,2048]{1,0:T(8,128)(2,1)}, u32[]{:S(2)}) copy-start(bf16[96,2048]{1,0:T(8,128)(2,1)} %base_ref.1) | copy-start | bytes 1179652
  13.1 1.1 copy-start.1
  14.3 26.1 %copy-start.5 = (bf16[2048]{0:T(1024)(128)(2,1)S(1)}, bf16[2048]{0:T(1024)(128)(2,1)}, u32[]{:S(2)}) copy-start(bf16[2048]{0:T(1024)(128)(2,1)} %param.13) | copy-start | bytes 12292
  40.4 1.4 copy-start.3
  173.3 1.1 copy-start.2
  199.0 1.4 copy-start

commit v3 on v2

--- a/solution.py
+++ b/solution.py
@@ -200,8 +200,8 @@
     )(code, dec, had)
 
 
-def ffn_body(n, chunks, cw, code_ref, dec_ref, gain_ref, had_ref, gate_ref, up_ref, h_ref,
-             x_ref, sq_ref, sqr_ref, w_ref, p_ref, r_ref,
+def ffn_body(n, chunks, cw, code_ref, dec_ref, gain_ref, had_ref, sign_ref, scale_ref, gate_ref, up_ref, down_ref, o_ref,
+             h_ref, down_held, acc_ref, down_sem, x_ref, sq_ref, sqr_ref, w_ref, p_ref, r_ref,
              w_sem, rs_send, rs_recv, ag_send, ag_recv, sq_send, sq_recv):
     z = lax.axis_index("request")
     half = p_ref.shape[2]
@@ -226,7 +226,12 @@
     for copy in weights(0, 0):
         copy.start()
 
+    down_copy = pltpu.make_async_copy(down_ref, down_held, down_sem)
+    down_copy.start()
     sq_ref[...] = jnp.zeros_like(sq_ref)
+    acc_ref[...] = jnp.zeros_like(acc_ref)
+    group = 2 if chunks % 2 == 0 else 1
+    tile = min(512, acc_ref.shape[2])
 
     @pl.loop(0, code_ref.shape[1] // 128)
     def _(b):
@@ -328,6 +333,29 @@
                 def _():
                     hidden_copy(d, back).start()
 
+        @pl.when(s == (n - 1) * LAG)
+        def _():
+            down_copy.wait()
+
+        for d in (0, 1):
+            back = s - (2 * (n - 1) - place[d]) * LAG
+
+            @pl.when((back >= 0) & (back < chunks) & (lax.rem(back, group) == group - 1))
+            def _(d=d, back=back):
+                units = pl.ds(pl.multiple_of((back - (group - 1)) * cw, cw), group * cw)
+                part = h_ref[pl.ds(d * half, half), units]
+
+                @pl.loop(0, acc_ref.shape[2] // tile)
+                def _(i):
+                    cols = pl.ds(pl.multiple_of(i * tile, tile), tile)
+                    acc_ref[d, :, cols] += jnp.dot(part, down_held[units, cols], preferred_element_type=jnp.float32)
+
+    @pl.loop(0, acc_ref.shape[2] // 128)
+    def _(b):
+        cols = pl.ds(pl.multiple_of(b * 128, 128), 128)
+        for d in (0, 1):
+            o_ref[pl.ds(d * half, half), cols] = encode(acc_ref[d, :, cols], sign_ref[:, cols], scale_ref[:, cols], had_ref[...])
+
     for d in (0, 1):
         pos = place[d]
 
@@ -346,7 +374,7 @@
                 hidden_copy(d, c).wait_send()
 
 
-def ffn(n, code, dec, gain, had, gate_weight, up_weight):
+def ffn(n, code, dec, gain, had, sign, scale, gate_weight, up_weight, down_weight):
     rows, depth = code.shape
     units = gate_weight.shape[1]
     cw = 128
@@ -355,10 +383,14 @@
     vmem = pl.BlockSpec(memory_space=pltpu.VMEM)
     return pl.pallas_call(
         functools.partial(ffn_body, n, chunks, cw),
-        out_shape=jax.ShapeDtypeStruct((rows, units), jnp.bfloat16),
-        in_specs=[vmem] * 4 + [pl.BlockSpec(memory_space=pl.ANY)] * 2,
+        out_shape=jax.ShapeDtypeStruct((rows, down_weight.shape[1]), jnp.bfloat16),
+        in_specs=[vmem] * 6 + [pl.BlockSpec(memory_space=pl.ANY)] * 3,
         out_specs=vmem,
         scratch_shapes=[
+            pltpu.VMEM((rows, units), jnp.bfloat16),
+            pltpu.VMEM(down_weight.shape, jnp.bfloat16),
+            pltpu.VMEM((2, half, down_weight.shape[1]), jnp.float32),
+            pltpu.SemaphoreType.DMA,
             pltpu.VMEM((rows, depth), jnp.bfloat16),
             pltpu.VMEM((2, half, 128), jnp.float32),
             pltpu.VMEM((2, half, 128), jnp.float32),
@@ -374,7 +406,7 @@
             pltpu.SemaphoreType.DMA((2,)),
         ],
         compiler_params=pltpu.CompilerParams(collective_id=0, has_side_effects=True, vmem_limit_bytes=VMEM_LIMIT),
-    )(code, dec, gain, had, gate_weight, up_weight)
+    )(code, dec, gain, had, sign, scale, gate_weight, up_weight, down_weight)
 
 
 def shards(n_tensor, n_request, attn_heads, out_weight, resid, gain, gate_weight, up_weight, down_weight, signs, expos):
@@ -387,8 +419,9 @@
 
     coded = project(attn_heads, out_weight, row(sign, 0), row(enc, 0), had)
     hidden_state, gathered = exchange(n_tensor, True, 1, coded, resid, row(dec, 0), row(sign, 1), row(enc, 1), had)
-    hidden = ffn(n_request, gathered, row(dec, 1), gain.astype(jnp.float32)[None, :], had, gate_weight, up_weight)
-    coded = project(hidden, down_weight, row(sign, 2), row(enc, 2), had)
+    coded = ffn(
+        n_request, gathered, row(dec, 1), gain.astype(jnp.float32)[None, :], had, row(sign, 2), row(enc, 2),
+        gate_weight, up_weight, down_weight)
     (gathered,) = exchange(n_tensor, False, 2, coded, hidden_state, row(dec, 2), row(sign, 3), row(enc, 3), had)
     return finish(gathered, row(dec, 3), had)
 

time: 204 us -> 193 us (0.946)
  Pallas kernels: 195 us -> 186 us
    pallas_call x2 -> x1, Pallas kernels: 23.9 us -> 10.5 us  [project(): pl.pallas_call(project_body, grid=(width // block,), in_specs=[pl.BlockSp...]
    pallas_call x1, Pallas kernels: 118 us -> 122 us  [ffn(): pl.pallas_call(functools.partial(ffn_body, n, chunks, cw), out_shape=jax....]
    unnamed x13 -> x11, local copies, waits for them, and re-layouts: 5.16 us -> 3.76 us
where the time goes in v3:
time: 193 us; the launch traced here: 192 us
  Pallas kernels  186 us (96%)
  local copies, waits for them, and re-layouts  4.09 us (2%)
  other arithmetic  2.41 us (1%)
    pallas_call x1, Pallas kernels, ffn(): pl.pallas_call(functools.partial(ffn_body, n, chunks, cw), out_shape=jax....  122 us
    pallas_call x2, Pallas kernels, exchange(): pl.pallas_call(functools.partial(exchange_body, nx, parts, keep), out_sha...  50.4 us
    pallas_call x1, Pallas kernels, project(): pl.pallas_call(project_body, grid=(width // block,), in_specs=[pl.BlockSp...  10.5 us

profile of v3, /device:TPU:0, one launch (start us, length us, event | category | flops | bytes accessed | tf_op | source)
XLA Modules:
  0.0 192.1 jit_solution(11724421891929417404)
XLA Ops:
  0.0 0.8 exponential_multiply_fusion
  0.8 0.1 broadcast_bitcast_fusion
  0.8 0.8 bitcast_multiply_fusion
  1.6 0.8 add_convert_fusion
  2.5 0.1 fusion.3.had_ref
  2.6 0.1 broadcast_in_dim.27
  2.6 0.0 copy-start.3
  2.6 10.5 %shard_map.100 = bf16[384,2048]{1,0:T(8,128)(2,1)S(1)} custom-call(bf16[384,2048]{1,0:T(8,128)(2,1)} %a_ref.1, bf16[2048,2048]{1,0:T(8,128)(2,1)} %w_ref.1, f32[1,2048]{1,0:T(1,128)S(1)} %get-tuple-element.23.sign_ref, f32[1,2048]{1,0:T(1,128)S(1)} %bitcast.28, bf16[128,128]{1,0:T(8,128)(2,1)S(1)} %fusion.3.had_ref), custom_call_target="tpu_custom_call" | custom-call | tf_op jit(solution)/shard_map/pallas_call | solution.py:50
  13.1 0.0 copy-start.2
  13.1 1.1 copy-done.2
  14.3 0.0 copy-start.4
  14.3 0.1 broadcast_in_dim.30
  14.4 0.0 copy-done.3
  14.4 26.0 %shard_map.101 = (f32[96,2048]{1,0:T(8,128)S(1)}, bf16[2,2,96,2048]{3,2,1,0:T(8,128)(2,1)}) custom-call(bf16[2,2,96,2048]{3,2,1,0:T(8,128)(2,1)} %bitcast.23, bf16[96,2048]{1,0:T(8,128)(2,1)S(1)} %copy-done.3, f32[1,2048]{1,0:T(1,128)S(1)} %get-tuple-element.12.dec_ref, f32[1,2048]{1,0:T(1,128)S(1)} %get-tuple-element.24.sign_ref, f32[1,2048]{1,0:T(1,128)S(1)} %bitcast.24, ...), custom_call_target="tpu_custom_call" | custom-call | tf_op jit(solution)/shard_map/pallas_call | solution.py:157
  40.4 0.1 broadcast_in_dim.34
  40.4 0.0 copy-done.4
  40.4 122.3 %shard_map.102 = bf16[384,2048]{1,0:T(8,128)(2,1)S(1)} custom-call(bf16[384,2048]{1,0:T(8,128)(2,1)} %bitcast.29, f32[1,2048]{1,0:T(1,128)S(1)} %get-tuple-element.11.dec_ref, f32[1,2048]{1,0:T(1,128)S(1)} %bitcast.27, bf16[128,128]{1,0:T(8,128)(2,1)S(1)} %fusion.3.had_ref, f32[1,2048]{1,0:T(1,128)S(1)} %get-tuple-element.25.sign_ref, ...), custom_call_target="tpu_custom_call" | custom-call | tf_op jit(solution)/shard_map/pallas_call | solution.py:384
  162.8 0.0 copy-start
  162.8 1.1 copy-done
  163.9 0.1 broadcast_in_dim.36
  164.0 24.4 %shard_map.103 = bf16[2,2,96,2048]{3,2,1,0:T(8,128)(2,1)} custom-call(bf16[2,2,96,2048]{3,2,1,0:T(8,128)(2,1)} %bitcast.21, f32[96,2048]{1,0:T(8,128)S(1)} %get-tuple-element.8.base_ref, f32[1,2048]{1,0:T(1,128)S(1)} %get-tuple-element.10.dec_ref, f32[1,2048]{1,0:T(1,128)S(1)} %get-tuple-element.26.sign_ref, f32[1,2048]{1,0:T(1,128)S(1)} %bitcast.26, ...), custom_call_target="tpu_custom_call" | custom-call | tf_op jit(solution)/shard_map/pallas_call | solution.py:157
  188.4 0.0 copy-start.1
  188.4 1.4 copy-done.1
  189.8 2.3 %shard_map.104 = bf16[384,2048]{1,0:T(8,128)(2,1)} custom-call(bf16[384,2048]{1,0:T(8,128)(2,1)S(1)} %bitcast.22, f32[1,2048]{1,0:T(1,128)S(1)} %get-tuple-element.9.dec_ref, bf16[128,128]{1,0:T(8,128)(2,1)S(1)} %fusion.3.had_ref), custom_call_target="tpu_custom_call" | custom-call | tf_op jit(solution)/shard_map/pallas_call | solution.py:189
  (3 shorter events, 0.1 us)
Async XLA Ops:
  2.6 11.7 %copy-start.3 = (bf16[96,2048]{1,0:T(8,128)(2,1)S(1)}, bf16[96,2048]{1,0:T(8,128)(2,1)}, u32[]{:S(2)}) copy-start(bf16[96,2048]{1,0:T(8,128)(2,1)} %base_ref.1) | copy-start | bytes 1179652
  13.1 1.1 copy-start.2
  14.3 26.1 %copy-start.4 = (bf16[2048]{0:T(1024)(128)(2,1)S(1)}, bf16[2048]{0:T(1024)(128)(2,1)}, u32[]{:S(2)}) copy-start(bf16[2048]{0:T(1024)(128)(2,1)} %param.13) | copy-start | bytes 12292
  162.8 1.1 copy-start
  188.4 1.4 copy-start.1

commit v4 on v3

--- a/solution.py
+++ b/solution.py
@@ -9,7 +9,7 @@
 
 D = 8192
 MESH = pl.DeviceIdType.MESH
-LAG = 2
+LAG = 1
 VMEM_LIMIT = 52 * 2**20
 
 

time: 193 us -> 216 us (1.12)
  Pallas kernels: 186 us -> 209 us
    pallas_call x1, Pallas kernels: 122 us -> 145 us  [ffn(): pl.pallas_call(functools.partial(ffn_body, n, chunks, cw), out_shape=jax....]
where the time goes in v4:
time: 216 us; the launch traced here: 215 us
  Pallas kernels  209 us (97%)
  local copies, waits for them, and re-layouts  4.09 us (2%)
  other arithmetic  2.41 us (1%)
    pallas_call x1, Pallas kernels, ffn(): pl.pallas_call(functools.partial(ffn_body, n, chunks, cw), out_shape=jax....  145 us
    pallas_call x2, Pallas kernels, exchange(): pl.pallas_call(functools.partial(exchange_body, nx, parts, keep), out_sha...  51.1 us
    pallas_call x1, Pallas kernels, project(): pl.pallas_call(project_body, grid=(width // block,), in_specs=[pl.BlockSp...  10.5 us

profile of v4, /device:TPU:0, one launch (start us, length us, event | category | flops | bytes accessed | tf_op | source)
XLA Modules:
  0.0 215.3 jit_solution(6962109149855939471)
XLA Ops:
  0.0 0.8 exponential_multiply_fusion
  0.8 0.1 broadcast_bitcast_fusion
  0.8 0.8 bitcast_multiply_fusion
  1.6 0.8 add_convert_fusion
  2.5 0.1 fusion.3.had_ref
  2.6 0.1 broadcast_in_dim.27
  2.6 0.0 copy-start.3
  2.6 10.5 %shard_map.100 = bf16[384,2048]{1,0:T(8,128)(2,1)S(1)} custom-call(bf16[384,2048]{1,0:T(8,128)(2,1)} %a_ref.1, bf16[2048,2048]{1,0:T(8,128)(2,1)} %w_ref.1, f32[1,2048]{1,0:T(1,128)S(1)} %get-tuple-element.23.sign_ref, f32[1,2048]{1,0:T(1,128)S(1)} %bitcast.28, bf16[128,128]{1,0:T(8,128)(2,1)S(1)} %fusion.3.had_ref), custom_call_target="tpu_custom_call" | custom-call | tf_op jit(solution)/shard_map/pallas_call | solution.py:50
  13.1 0.0 copy-start.2
  13.1 1.1 copy-done.2
  14.3 0.0 copy-start.4
  14.3 0.1 broadcast_in_dim.30
  14.4 0.0 copy-done.3
  14.4 26.0 %shard_map.101 = (f32[96,2048]{1,0:T(8,128)S(1)}, bf16[2,2,96,2048]{3,2,1,0:T(8,128)(2,1)}) custom-call(bf16[2,2,96,2048]{3,2,1,0:T(8,128)(2,1)} %bitcast.23, bf16[96,2048]{1,0:T(8,128)(2,1)S(1)} %copy-done.3, f32[1,2048]{1,0:T(1,128)S(1)} %get-tuple-element.12.dec_ref, f32[1,2048]{1,0:T(1,128)S(1)} %get-tuple-element.24.sign_ref, f32[1,2048]{1,0:T(1,128)S(1)} %bitcast.24, ...), custom_call_target="tpu_custom_call" | custom-call | tf_op jit(solution)/shard_map/pallas_call | solution.py:157
  40.4 0.1 broadcast_in_dim.34
  40.4 0.0 copy-done.4
  40.4 144.8 %shard_map.102 = bf16[384,2048]{1,0:T(8,128)(2,1)S(1)} custom-call(bf16[384,2048]{1,0:T(8,128)(2,1)} %bitcast.29, f32[1,2048]{1,0:T(1,128)S(1)} %get-tuple-element.11.dec_ref, f32[1,2048]{1,0:T(1,128)S(1)} %bitcast.27, bf16[128,128]{1,0:T(8,128)(2,1)S(1)} %fusion.3.had_ref, f32[1,2048]{1,0:T(1,128)S(1)} %get-tuple-element.25.sign_ref, ...), custom_call_target="tpu_custom_call" | custom-call | tf_op jit(solution)/shard_map/pallas_call | solution.py:384
  185.2 0.0 copy-start
  185.2 1.1 copy-done
  186.4 0.1 broadcast_in_dim.36
  186.4 25.1 %shard_map.103 = bf16[2,2,96,2048]{3,2,1,0:T(8,128)(2,1)} custom-call(bf16[2,2,96,2048]{3,2,1,0:T(8,128)(2,1)} %bitcast.21, f32[96,2048]{1,0:T(8,128)S(1)} %get-tuple-element.8.base_ref, f32[1,2048]{1,0:T(1,128)S(1)} %get-tuple-element.10.dec_ref, f32[1,2048]{1,0:T(1,128)S(1)} %get-tuple-element.26.sign_ref, f32[1,2048]{1,0:T(1,128)S(1)} %bitcast.26, ...), custom_call_target="tpu_custom_call" | custom-call | tf_op jit(solution)/shard_map/pallas_call | solution.py:157
  211.5 0.0 copy-start.1
  211.5 1.4 copy-done.1
  212.9 2.3 %shard_map.104 = bf16[384,2048]{1,0:T(8,128)(2,1)} custom-call(bf16[384,2048]{1,0:T(8,128)(2,1)S(1)} %bitcast.22, f32[1,2048]{1,0:T(1,128)S(1)} %get-tuple-element.9.dec_ref, bf16[128,128]{1,0:T(8,128)(2,1)S(1)} %fusion.3.had_ref), custom_call_target="tpu_custom_call" | custom-call | tf_op jit(solution)/shard_map/pallas_call | solution.py:189
  (3 shorter events, 0.1 us)
Async XLA Ops:
  2.6 11.7 %copy-start.3 = (bf16[96,2048]{1,0:T(8,128)(2,1)S(1)}, bf16[96,2048]{1,0:T(8,128)(2,1)}, u32[]{:S(2)}) copy-start(bf16[96,2048]{1,0:T(8,128)(2,1)} %base_ref.1) | copy-start | bytes 1179652
  13.1 1.1 copy-start.2
  14.3 26.1 %copy-start.4 = (bf16[2048]{0:T(1024)(128)(2,1)S(1)}, bf16[2048]{0:T(1024)(128)(2,1)}, u32[]{:S(2)}) copy-start(bf16[2048]{0:T(1024)(128)(2,1)} %param.13) | copy-start | bytes 12292
  185.2 1.1 copy-start
  211.5 1.4 copy-start.1

commit v5 on v3

--- a/solution.py
+++ b/solution.py
@@ -36,36 +36,15 @@
     return jnp.dot(codes, had, preferred_element_type=jnp.float32) * scale
 
 
-def project_body(a_ref, w_ref, sign_ref, scale_ref, had_ref, o_ref):
-    product = jnp.dot(a_ref[...], w_ref[...], preferred_element_type=jnp.float32)
-    for low in range(0, product.shape[1], 128):
-        cols = slice(low, low + 128)
-        o_ref[:, cols] = encode(product[:, cols], sign_ref[:, cols], scale_ref[:, cols], had_ref[...])
-
-
-def project(a, w, sign, scale, had):
-    rows, depth = a.shape
-    width = w.shape[1]
-    block = 256
-    return pl.pallas_call(
-        project_body,
-        grid=(width // block,),
-        in_specs=[
-            pl.BlockSpec((rows, depth), lambda j: (0, 0)),
-            pl.BlockSpec((depth, block), lambda j: (0, j)),
-            pl.BlockSpec((1, block), lambda j: (0, j)),
-            pl.BlockSpec((1, block), lambda j: (0, j)),
-            pl.BlockSpec((128, 128), lambda j: (0, 0)),
-        ],
-        out_specs=pl.BlockSpec((rows, block), lambda j: (0, j)),
-        out_shape=jax.ShapeDtypeStruct((rows, width), jnp.bfloat16),
-        compiler_params=pltpu.CompilerParams(vmem_limit_bytes=VMEM_LIMIT),
-    )(a, w, sign, scale, had)
-
-
-def exchange_body(nx, parts, keep, code_ref, base_ref, dec_ref, sign_ref, scale_ref, had_ref, *refs):
+def exchange_body(nx, parts, keep, *refs):
+    if keep:
+        a_ref, w_ref, first_sign, first_scale, *refs = refs
+    else:
+        code_ref, *refs = refs
+    base_ref, dec_ref, sign_ref, scale_ref, had_ref, *refs = refs
     if keep:
         state_ref, *refs = refs
+        *refs, code_ref, w_held, w_sem = refs
     (o_ref, s_ref, q_ref, g_ref, pair_send, pair_recv, sum_send, sum_recv, out_send, out_recv, fwd_send, fwd_recv) = refs
     t = lax.axis_index("tensor")
     core = lax.rem(t, 2)
@@ -106,21 +85,49 @@
             src_ref=part, dst_ref=part, send_sem=fwd_send.at[k, j], recv_sem=fwd_recv.at[k, j],
             device_id={"tensor": sibling}, device_id_type=MESH)
 
+    def weight_copy(j):
+        return pltpu.make_async_copy(w_ref.at[:, cols(j)], w_held.at[:, cols(j)], w_sem.at[j])
+
+    def produce(j):
+        weight_copy(j).wait()
+        tile = min(width, 256)
+        own = code_ref.shape[2]
+
+        @pl.loop(0, width // tile)
+        def _(i):
+            start = pl.multiple_of(j * width + i * tile, 128)
+            product = jnp.dot(a_ref[...], w_held[:, pl.ds(start, tile)], preferred_element_type=jnp.float32)
+            for low in range(0, tile, 128):
+                here = pl.ds(pl.multiple_of(start + low, 128), 128)
+                turned = turn(product[:, low:low + 128] * first_sign[:, here], had_ref[...]) * first_scale[:, here]
+                turned = jnp.clip(turned, -448.0, 448.0)
+                for to in range(2 * nx):
+                    code_ref[to // 2, to % 2, :, here] = turned[to * own:(to + 1) * own].astype(jnp.bfloat16)
+
+    if keep:
+        for j in range(parts):
+            weight_copy(j).start()
     barrier = pltpu.get_barrier_semaphore()
     pl.semaphore_signal(barrier, inc=1, device_id={"tensor": sibling}, device_id_type=MESH)
     for k in range(1, nx):
         pl.semaphore_signal(barrier, inc=1, device_id={"tensor": chip_at(k) * 2 + core}, device_id_type=MESH)
     pl.semaphore_wait(barrier, nx)
 
-    for j in range(parts):
-        pair_copy(j).start()
-    for j in range(parts):
+    def add_pair(j):
         pair_copy(j).wait_recv()
         for chip_to in range(nx):
             both = code_ref[chip_to, core, :, span(j)].astype(jnp.float32) + s_ref[chip_to, :, span(j)].astype(jnp.float32)
             q_ref[chip_to, :, span(j)] = both.astype(jnp.bfloat16)
         for k in range(1, nx):
             sum_copy(k, j).start()
+
+    for j in range(parts):
+        if keep:
+            produce(j)
+        pair_copy(j).start()
+        if j > 0:
+            add_pair(j - 1)
+    add_pair(parts - 1)
     for j in range(parts):
         total = q_ref[chip, :, span(j)].astype(jnp.float32)
         for k in range(1, nx):
@@ -149,15 +156,15 @@
             out_copy(k, j).wait_send()
 
 
-def exchange(n_tensor, keep, name, code, base, dec, sign, scale, had):
-    rows, width = code.shape
+def exchange(n_tensor, keep, name, first, base, dec, sign, scale, had):
+    rows, width = first[0].shape[0], base.shape[1]
     nx, own, parts = n_tensor // 2, rows // n_tensor, 4
     vmem = pl.BlockSpec(memory_space=pltpu.VMEM)
     states = [jax.ShapeDtypeStruct((own, width), jnp.float32)] if keep else []
     *state, out = pl.pallas_call(
         functools.partial(exchange_body, nx, parts, keep),
         out_shape=states + [jax.ShapeDtypeStruct((nx, 2, own, width), jnp.bfloat16)],
-        in_specs=[vmem] * 6,
+        in_specs=([vmem, pl.BlockSpec(memory_space=pl.ANY), vmem, vmem] if keep else [vmem]) + [vmem] * 5,
         out_specs=[vmem] * (len(states) + 1),
         scratch_shapes=[
             pltpu.VMEM((nx, own, width), jnp.bfloat16),
@@ -171,9 +178,13 @@
             pltpu.SemaphoreType.DMA((nx - 1, parts)),
             pltpu.SemaphoreType.DMA((nx, parts)),
             pltpu.SemaphoreType.DMA((nx, parts)),
-        ],
+        ] + ([
+            pltpu.VMEM((nx, 2, own, width), jnp.bfloat16),
+            pltpu.VMEM(first[1].shape, jnp.bfloat16),
+            pltpu.SemaphoreType.DMA((parts,)),
+        ] if keep else []),
         compiler_params=pltpu.CompilerParams(collective_id=name, has_side_effects=True, vmem_limit_bytes=VMEM_LIMIT),
-    )(code.reshape(nx, 2, own, width), base, dec, sign, scale, had)
+    )(*(first if keep else [first[0].reshape(nx, 2, own, width)]), base, dec, sign, scale, had)
     return (*state, out.reshape(rows, width))
 
 
@@ -417,12 +428,12 @@
     dec = jnp.repeat(0.0625 * jnp.exp2(shift.astype(jnp.float32)), 128, axis=1) * sign
     row = lambda table, k: table[k:k + 1]
 
-    coded = project(attn_heads, out_weight, row(sign, 0), row(enc, 0), had)
-    hidden_state, gathered = exchange(n_tensor, True, 1, coded, resid, row(dec, 0), row(sign, 1), row(enc, 1), had)
+    first = (attn_heads, out_weight, row(sign, 0), row(enc, 0))
+    hidden_state, gathered = exchange(n_tensor, True, 1, first, resid, row(dec, 0), row(sign, 1), row(enc, 1), had)
     coded = ffn(
         n_request, gathered, row(dec, 1), gain.astype(jnp.float32)[None, :], had, row(sign, 2), row(enc, 2),
         gate_weight, up_weight, down_weight)
-    (gathered,) = exchange(n_tensor, False, 2, coded, hidden_state, row(dec, 2), row(sign, 3), row(enc, 3), had)
+    (gathered,) = exchange(n_tensor, False, 2, (coded,), hidden_state, row(dec, 2), row(sign, 3), row(enc, 3), had)
     return finish(gathered, row(dec, 3), had)
 
 

time: 193 us -> 185 us (0.959)
  Pallas kernels: 186 us -> 178 us
    pallas_call x1 -> x0, Pallas kernels: 10.5 us -> none  [project(): pl.pallas_call(project_body, grid=(width // block,), in_specs=[pl.BlockSp...]
    pallas_call x2, Pallas kernels: 50.4 us -> 53.9 us  [exchange(): pl.pallas_call(functools.partial(exchange_body, nx, parts, keep), out_sha...]
where the time goes in v5:
time: 185 us; the launch traced here: 184 us
  Pallas kernels  178 us (96%)
  local copies, waits for them, and re-layouts  3.94 us (2%)
  other arithmetic  2.41 us (1%)
    pallas_call x1, Pallas kernels, ffn(): pl.pallas_call(functools.partial(ffn_body, n, chunks, cw), out_shape=jax....  122 us
    pallas_call x2, Pallas kernels, exchange(): pl.pallas_call(functools.partial(exchange_body, nx, parts, keep), out_sha...  53.9 us

profile of v5, /device:TPU:0, one launch (start us, length us, event | category | flops | bytes accessed | tf_op | source)
XLA Modules:
  0.0 184.4 jit_solution(11319834239885275058)
XLA Ops:
  0.0 0.8 exponential_multiply_fusion
  0.8 0.1 broadcast_bitcast_fusion
  0.8 0.8 bitcast_multiply_fusion
  1.6 0.8 add_convert_fusion
  2.5 0.1 broadcast_in_dim.27
  2.5 0.1 broadcast_in_dim.30
  2.6 0.1 fusion.3.refs_8_.had_ref.refs_5_
  2.7 0.0 copy-start.2
  2.7 1.0 copy-done.2
  3.7 0.0 copy-start.3
  3.7 29.9 %shard_map.100 = (f32[96,2048]{1,0:T(8,128)S(1)}, bf16[2,2,96,2048]{3,2,1,0:T(8,128)(2,1)}) custom-call(bf16[384,2048]{1,0:T(8,128)(2,1)} %refs_0_.1, bf16[2048,2048]{1,0:T(8,128)(2,1)} %refs_1_.1, f32[1,2048]{1,0:T(1,128)S(1)} %get-tuple-element.23.refs_2_, f32[1,2048]{1,0:T(1,128)S(1)} %bitcast.25, bf16[96,2048]{1,0:T(8,128)(2,1)S(1)} %copy-done.2, ...), custom_call_target="tpu_custom_call" | custom-call | tf_op jit(solution)/shard_map/pallas_call | solution.py:164
  33.6 0.1 broadcast_in_dim.34
  33.7 0.0 copy-done.3
  33.7 121.8 %shard_map.101 = bf16[384,2048]{1,0:T(8,128)(2,1)S(1)} custom-call(bf16[384,2048]{1,0:T(8,128)(2,1)} %bitcast.27, f32[1,2048]{1,0:T(1,128)S(1)} %get-tuple-element.11.dec_ref, f32[1,2048]{1,0:T(1,128)S(1)} %bitcast.24, bf16[128,128]{1,0:T(8,128)(2,1)S(1)} %fusion.3.refs_8_.had_ref.refs_5_, f32[1,2048]{1,0:T(1,128)S(1)} %get-tuple-element.25.sign_ref, ...), custom_call_target="tpu_custom_call" | custom-call | tf_op jit(solution)/shard_map/pallas_call | solution.py:395
  155.4 0.0 copy-start
  155.4 1.1 copy-done
  156.6 0.1 broadcast_in_dim.36
  156.6 24.0 %shard_map.102 = bf16[2,2,96,2048]{3,2,1,0:T(8,128)(2,1)} custom-call(bf16[2,2,96,2048]{3,2,1,0:T(8,128)(2,1)} %bitcast.20, f32[96,2048]{1,0:T(8,128)S(1)} %get-tuple-element.8.refs_1_, f32[1,2048]{1,0:T(1,128)S(1)} %get-tuple-element.10.refs_2_, f32[1,2048]{1,0:T(1,128)S(1)} %get-tuple-element.26.refs_3_, f32[1,2048]{1,0:T(1,128)S(1)} %bitcast.23, ...), custom_call_target="tpu_custom_call" | custom-call | tf_op jit(solution)/shard_map/pallas_call | solution.py:164
  180.6 0.0 copy-start.1
  180.7 1.4 copy-done.1
  182.1 2.3 %shard_map.103 = bf16[384,2048]{1,0:T(8,128)(2,1)} custom-call(bf16[384,2048]{1,0:T(8,128)(2,1)S(1)} %bitcast.21, f32[1,2048]{1,0:T(1,128)S(1)} %get-tuple-element.9.dec_ref, bf16[128,128]{1,0:T(8,128)(2,1)S(1)} %fusion.3.refs_8_.had_ref.refs_5_), custom_call_target="tpu_custom_call" | custom-call | tf_op jit(solution)/shard_map/pallas_call | solution.py:200
  (3 shorter events, 0.1 us)
Async XLA Ops:
  2.7 1.0 copy-start.2
  3.7 30.0 %copy-start.3 = (bf16[2048]{0:T(1024)(128)(2,1)S(1)}, bf16[2048]{0:T(1024)(128)(2,1)}, u32[]{:S(2)}) copy-start(bf16[2048]{0:T(1024)(128)(2,1)} %param.13) | copy-start | bytes 12292
  155.4 1.1 copy-start
  180.6 1.4 copy-start.1
